TPU v7x, 32 devices: a whole 2x2x4 slice. The times are simulated.
32 devices in a mesh: col: 4 (over x, core), grp: 8 (over z, y).
Axes of the slice: x: 2, y: 2, z: 4, core: 2. Of those that a mesh axis runs over, the one named last changes fastest.
Arguments:
- grid_fields: bfloat16 [1024, 512], P(('col', 'grp')), may hold values from -6 to 6
- brick_slot: int32 [1024], P('col'), may hold values from 0 to 255, as said below
- block_brick: int32 [1024], P(('col', 'grp')), may hold values from 0 to 287, as said below
- node_mask: int32 [1024, 64], P(('col', 'grp')), may hold values 0 or 1
- counts: int32 [1024], P(('col', 'grp')), may hold values from 1 to 128, as said below
- shape_t: bfloat16 [1024, 64, 128], P(('col', 'grp')), may hold values from 0 to 0.099609375
- part_mass: float32 [1024, 128], P(('col', 'grp')), may hold values from 0.5 to 2
- part_vel: float32 [1024, 3, 128], P(('col', 'grp')), may hold values from -6 to 6
Outputs:
- vel_new: float32 [1024, 3, 128], P(('col', 'grp'))
- grid_momentum: float32 [1024, 256], P(('col', 'grp'))
Inputs may be any that keep to these rules, and one draw needn't show every extreme that they name: `brick_slot`: each aligned run of 256 entries is a permutation of 0 .. 255. `block_brick`: the first block of each device refers to a left neighbour brick, the second to a right neighbour brick, all others to bricks of the column itself; of one device's blocks at most 4 refer to bricks stored on any one device of the column, and exactly 4 to some device. `counts`: the first block of each device is full.
All inputs are finite; a program needn't handle non-finite values. No bound on the sum of `node_mask` on one device may be relied on, other than what follows from the above.
Results may differ from a plain program's by a relative error of at most 0.00041.
Values may be sent and summed in bfloat16 or wider, within the bound.
A program may use at most 64 MiB of HBM per device.

v0:
```python
import jax
import jax.numpy as jnp
from jax import lax
from jax.sharding import PartitionSpec as P

NODES = 64
FIELDS = 8
OUTF = 4
PBLK = 128
RIM = 16


def with_halo(cells, sides, width):
    for axis, dim in sides:
        count = lax.axis_size(axis)
        ends = count - 1
        head = lax.slice_in_dim(cells, 0, width, axis=dim)
        tail = lax.slice_in_dim(cells, cells.shape[dim] - width, cells.shape[dim], axis=dim)
        cells = jnp.concatenate(
            [
                lax.ppermute(tail, axis, [(i, (i + 1) % count) for i in range(ends)]),
                cells,
                lax.ppermute(head, axis, [((i + 1) % count, i) for i in range(ends)]),
            ],
            axis=dim,
        )
    return cells


def local(grid_fields, brick_slot, block_brick, node_mask, counts, shape_t, part_mass, part_vel):
    columns = brick_slot.shape[0]
    blocks = block_brick.shape[0]
    local_rows = grid_fields.shape[0]
    groups = lax.axis_size("grp")
    slots_each = max(2, (blocks - 2 + groups - 1) // groups)
    own_index = block_brick - RIM
    is_own = (own_index >= 0) & (own_index < columns)
    own_slot = jnp.take(brick_slot, jnp.clip(own_index, 0, columns - 1))
    owner = jnp.where(is_own, own_slot // local_rows, -1)
    row_at = own_slot % local_rows
    order = jnp.arange(blocks, dtype=jnp.int32)
    earlier = (owner[:, None] == owner[None, :]) & (order[None, :] < order[:, None])
    rank = jnp.sum(earlier.astype(jnp.int32), axis=1)
    dest = jnp.where(is_own, owner * slots_each + rank, groups * slots_each)
    edge_ids = jnp.concatenate(
        [jnp.arange(RIM, dtype=jnp.int32), jnp.arange(columns - RIM, columns, dtype=jnp.int32)]
    )
    edge_slot = jnp.take(brick_slot, edge_ids)
    mine = edge_slot // local_rows == lax.axis_index("grp")
    edge_match = mine[:, None] & (
        (edge_slot % local_rows)[:, None] == jnp.arange(local_rows, dtype=jnp.int32)[None, :]
    )
    gathered = lax.all_gather(grid_fields, "grp", axis=0, tiled=True)
    logical = jnp.take(gathered, brick_slot, axis=0)
    rims = jnp.concatenate([logical[:RIM], logical[columns - RIM :]], axis=0)
    wider = with_halo(rims, (("col", 0),), RIM)
    left_in = wider[:RIM]
    right_in = wider[3 * RIM :]
    extended = jnp.concatenate([left_in, logical, right_in], axis=0)
    block_rows = jnp.take(extended, block_brick, axis=0)
    weights = shape_t * node_mask[:, :, None].astype(jnp.bfloat16)
    block_fields = block_rows.reshape(blocks, FIELDS, NODES)
    interp = jnp.einsum("bfn,bnp->bfp", block_fields, weights, preferred_element_type=jnp.float32)
    live = (jnp.arange(PBLK, dtype=jnp.int32)[None, :] < counts[:, None]).astype(jnp.float32)
    blend = 0.4 * interp[:, 0:3] + 0.6 * (part_vel + interp[:, 3:6])
    vel_next = blend / (1.0 + 0.5 * interp[:, 7:8] * interp[:, 7:8]) * live[:, None, :]
    first = part_mass * (1.0 + 0.5 * jnp.tanh(interp[:, 6])) * live
    contrib = jnp.concatenate([first[:, None, :], part_mass[:, None, :] * vel_next], axis=1).astype(
        jnp.bfloat16
    )
    partial_value = jnp.einsum("bfp,bnp->bfn", contrib, weights, preferred_element_type=jnp.float32)
    partial_value = partial_value.reshape(blocks, OUTF * NODES)
    rim_index = jnp.where(block_brick < RIM, block_brick, block_brick - columns)
    rim_hit = (
        (jnp.arange(2 * RIM, dtype=jnp.int32)[:, None] == rim_index[None, :]) & (~is_own)[None, :]
    ).astype(jnp.float32)
    outgoing = jnp.dot(
        rim_hit, partial_value, precision=lax.Precision.HIGHEST, preferred_element_type=jnp.float32
    )
    incoming = with_halo(outgoing, (("col", 0),), RIM)
    edge_in = jnp.concatenate([incoming[:RIM], incoming[3 * RIM :]], axis=0)
    totals = lax.psum(edge_in, "grp")
    send_rows = (
        jnp.zeros((groups * slots_each, OUTF * NODES), jnp.float32)
        .at[dest]
        .set(partial_value, mode="drop")
    )
    send_index = jnp.full((groups * slots_each,), -1, jnp.int32).at[dest].set(row_at, mode="drop")
    got_rows, got_index = (
        lax.all_to_all(
            send_rows.reshape(groups, slots_each, OUTF * NODES),
            "grp",
            split_axis=0,
            concat_axis=0,
            tiled=True,
        ),
        lax.all_to_all(
            send_index.reshape(groups, slots_each), "grp", split_axis=0, concat_axis=0, tiled=True
        ),
    )
    place = (
        jnp.arange(local_rows, dtype=jnp.int32)[:, None] == got_index.reshape(-1)[None, :]
    ).astype(jnp.float32)
    momentum = jnp.dot(
        place,
        got_rows.reshape(groups * slots_each, OUTF * NODES),
        precision=lax.Precision.HIGHEST,
        preferred_element_type=jnp.float32,
    )
    momentum = momentum + jnp.dot(
        edge_match.astype(jnp.float32).T,
        totals,
        precision=lax.Precision.HIGHEST,
        preferred_element_type=jnp.float32,
    )
    return (vel_next, momentum)


def solution(mesh):
    placed = (
        P(("col", "grp"), None),
        P("col"),
        P(("col", "grp")),
        P(("col", "grp"), None),
        P(("col", "grp")),
        P(("col", "grp"), None, None),
        P(("col", "grp"), None),
        P(("col", "grp"), None, None),
    )
    return jax.shard_map(
        local,
        mesh=mesh,
        in_specs=placed,
        out_specs=(P(("col", "grp"), None, None), P(("col", "grp"), None)),
        check_vma=False,
    )
```

profile of v0, /device:TPU:2, one launch (start us, length us, event | category | flops | bytes accessed | tf_op | source)
XLA Modules:
  0.0 105.9 jit_solution(12257198432379632999)
XLA Ops:
  0.6 0.7 compare_select_fusion
  1.4 31.3 %all_gather.3 = bf16[256,512]{1,0:T(8,128)(2,1)S(1)} all-gather(bf16[32,512]{1,0:T(8,128)(2,1)} %param.10), channel_id=1, replica_groups=mesh['col'=4,'grp'=8] {'grp'}, dimensions={0}, use_global_device_ids=true | all-gather | bytes 294912 | tf_op jit(solution)/shard_map/all_gather | solution.py:53
  32.7 1.2 %gather_fusion = bf16[256,512]{1,0:T(8,128)(2,1)S(1)} fusion(bf16[256,512]{1,0:T(8,128)(2,1)S(1)} %all_gather.3, s32[1024]{0:T(1024)S(1)} %pad_clamp_fusion.3), kind=kCustom, calls=%fused_computation.2 | custom fusion | bytes 525312 | tf_op jit(solution)/shard_map/jit(_take)/gather | solution.py:54
  34.0 1.9 %collective-permute-start = (bf16[16,512]{1,0:T(8,128)(2,1)S(1)}, bf16[16,512]{1,0:T(8,128)(2,1)S(1)}, u32[]{:S(2)}, u32[]{:S(2)}) collective-permute-start(bf16[16,512]{1,0:T(8,128)(2,1)S(1)} %get-tuple-element.17), channel_id=1, source_target_pairs={{0,8},{8,16},{16,24},{1,9},{9,17},{17,25},{2,10},{10,18},{18,26},{... | collective-permute-start | bytes 49160 | tf_op jit(solution)/shard_map/ppermute | solution.py:21
  35.9 3.6 %collective-permute-start.1 = (bf16[16,512]{1,0:T(8,128)(2,1)S(1)}, bf16[16,512]{1,0:T(8,128)(2,1)S(1)}, u32[]{:S(2)}, u32[]{:S(2)}) collective-permute-start(bf16[16,512]{1,0:T(8,128)(2,1)S(1)} %get-tuple-element.18), channel_id=1, source_target_pairs={{8,0},{16,8},{24,16},{9,1},{17,9},{25,17},{10,2},{18,10},{26,18},{... | collective-permute-start | bytes 49160 | tf_op jit(solution)/shard_map/ppermute | solution.py:23
  39.6 0.7 gather_fusion.2
  40.5 0.7 scatter_custom_fusion
  41.2 0.7 all_to_all.9
  41.9 5.6 %all-to-all-start = ((s32[8,1,4]{2,1,0:T(1,128)}), s32[8,1,4]{2,1,0:T(1,128)S(1)}, u32[]{:S(2)}, u32[]{:S(2)}) async-start(s32[8,1,4]{2,1,0:T(1,128)} %bitcast.1), calls=%async_computation | async-start | bytes 8192 | tf_op jit(solution)/shard_map/all_to_all | solution.py:97
  47.5 0.6 copy-done.5
  48.3 0.7 gather_fusion.3
  49.2 0.6 gather_fusion.1
  50.1 0.7 fusion.2
  50.8 0.6 copy-done.1
  52.4 1.9 %collective-permute-start.2 = (f32[16,256]{1,0:T(8,128)S(1)}, f32[16,256]{1,0:T(8,128)S(1)}, u32[]{:S(2)}, u32[]{:S(2)}) collective-permute-start(f32[16,256]{1,0:T(8,128)S(1)} %get-tuple-element.21), channel_id=1, source_target_pairs={{0,8},{8,16},{16,24},{1,9},{9,17},{17,25},{2,10},{10,18},{18,26},{... | collective-permute-start | bytes 49160 | tf_op jit(solution)/shard_map/ppermute | solution.py:21
  54.4 3.6 %collective-permute-start.3 = (f32[16,256]{1,0:T(8,128)S(1)}, f32[16,256]{1,0:T(8,128)S(1)}, u32[]{:S(2)}, u32[]{:S(2)}) collective-permute-start(f32[16,256]{1,0:T(8,128)S(1)} %get-tuple-element.22), channel_id=1, source_target_pairs={{8,0},{16,8},{24,16},{9,1},{17,9},{25,17},{10,2},{18,10},{26,18},{... | collective-permute-start | bytes 49160 | tf_op jit(solution)/shard_map/ppermute | solution.py:23
  58.0 0.5 broadcast.117
  58.6 0.7 reduce.3
  59.3 0.7 scatter_custom_fusion.1
  60.0 0.6 reshape.74
  60.7 6.0 %all-to-all-start.1 = ((f32[8,4,256]{2,1,0:T(4,128)}), f32[8,4,256]{2,1,0:T(4,128)S(1)}, u32[]{:S(2)}, u32[]{:S(2)}) async-start(f32[8,4,256]{2,1,0:T(4,128)} %reshape.74), calls=%async_computation.1 | async-start | bytes 65536 | tf_op jit(solution)/shard_map/all_to_all | solution.py:90
  66.7 0.6 copy.23
  67.3 37.6 %psum.7 = f32[32,256]{1,0:T(8,128)S(1)} all-reduce(f32[32,256]{1,0:T(8,128)S(1)} %pad_maximum_fusion.1), channel_id=1, replica_groups=mesh['col'=4,'grp'=8] {'grp'}, use_global_device_ids=true, to_apply=%region_3.5 | all-reduce | flops 8192 | bytes 65536 | tf_op jit(solution)/shard_map/psum | solution.py:82
  105.0 0.9 convolution_add_fusion
  (52 shorter events, 2.2 us)
Async XLA Ops:
  0.6 0.8 copy-start
  34.0 5.6 %copy-start.4 = (s32[32]{0:T(128)S(1)}, s32[32]{0:T(128)}, u32[]{:S(2)}) copy-start(s32[32]{0:T(128)} %param.12) | copy-start | bytes 388
  34.0 15.2 %collective-permute-start = (bf16[16,512]{1,0:T(8,128)(2,1)S(1)}, bf16[16,512]{1,0:T(8,128)(2,1)S(1)}, u32[]{:S(2)}, u32[]{:S(2)}) collective-permute-start(bf16[16,512]{1,0:T(8,128)(2,1)S(1)} %get-tuple-element.17), channel_id=1, source_target_pairs={{0,8},{8,16},{16,24},{1,9},{9,17},{17,25},{2,10},{10,18},{18,26},{... | collective-permute-start | bytes 49160 | tf_op jit(solution)/shard_map/ppermute | solution.py:21
  35.9 13.3 %collective-permute-start.1 = (bf16[16,512]{1,0:T(8,128)(2,1)S(1)}, bf16[16,512]{1,0:T(8,128)(2,1)S(1)}, u32[]{:S(2)}, u32[]{:S(2)}) collective-permute-start(bf16[16,512]{1,0:T(8,128)(2,1)S(1)} %get-tuple-element.18), channel_id=1, source_target_pairs={{8,0},{16,8},{24,16},{9,1},{17,9},{25,17},{10,2},{18,10},{26,18},{... | collective-permute-start | bytes 49160 | tf_op jit(solution)/shard_map/ppermute | solution.py:23
  41.9 16.1 %all-to-all-start = ((s32[8,1,4]{2,1,0:T(1,128)}), s32[8,1,4]{2,1,0:T(1,128)S(1)}, u32[]{:S(2)}, u32[]{:S(2)}) async-start(s32[8,1,4]{2,1,0:T(1,128)} %bitcast.1), calls=%async_computation | async-start | bytes 8192 | tf_op jit(solution)/shard_map/all_to_all | solution.py:97
  47.5 0.7 copy-start.5
  48.3 0.8 copy-start.3
  49.0 1.0 copy-start.6
  50.7 0.7 copy-start.1
  50.8 0.8 copy-start.2
  52.4 14.8 %collective-permute-start.2 = (f32[16,256]{1,0:T(8,128)S(1)}, f32[16,256]{1,0:T(8,128)S(1)}, u32[]{:S(2)}, u32[]{:S(2)}) collective-permute-start(f32[16,256]{1,0:T(8,128)S(1)} %get-tuple-element.21), channel_id=1, source_target_pairs={{0,8},{8,16},{16,24},{1,9},{9,17},{17,25},{2,10},{10,18},{18,26},{... | collective-permute-start | bytes 49160 | tf_op jit(solution)/shard_map/ppermute | solution.py:21
  54.4 12.9 %collective-permute-start.3 = (f32[16,256]{1,0:T(8,128)S(1)}, f32[16,256]{1,0:T(8,128)S(1)}, u32[]{:S(2)}, u32[]{:S(2)}) collective-permute-start(f32[16,256]{1,0:T(8,128)S(1)} %get-tuple-element.22), channel_id=1, source_target_pairs={{8,0},{16,8},{24,16},{9,1},{17,9},{25,17},{10,2},{18,10},{26,18},{... | collective-permute-start | bytes 49160 | tf_op jit(solution)/shard_map/ppermute | solution.py:23
  60.7 44.2 %all-to-all-start.1 = ((f32[8,4,256]{2,1,0:T(4,128)}), f32[8,4,256]{2,1,0:T(4,128)S(1)}, u32[]{:S(2)}, u32[]{:S(2)}) async-start(f32[8,4,256]{2,1,0:T(4,128)} %reshape.74), calls=%async_computation.1 | async-start | bytes 65536 | tf_op jit(solution)/shard_map/all_to_all | solution.py:90
where the time goes:
time: 106 us
  blocking collectives  68.9 us (65%)
  starting transfers between devices  22.7 us (21%)
  local copies, waits for them, and re-layouts  8.86 us (8%)
  matrix products  2.29 us (2%)
  other arithmetic  2.28 us (2%)
    psum x1, blocking collectives, local(): totals = lax.psum(edge_in, 'grp')  37.6 us
    all_gather x1, blocking collectives, local(): gathered = lax.all_gather(grid_fields, 'grp', axis=0, tiled=True)  31.3 us
    ppermute x2, starting transfers between devices, with_halo(): lax.ppermute(head, axis, [((i + 1) % count, i) for i in range(ends)])  7.28 us
    all_to_all x1, starting transfers between devices, local(): lax.all_to_all(send_rows.reshape(groups, slots_each, OUTF * NODES), 'grp'...  6 us
    all_to_all x1, starting transfers between devices, local(): lax.all_to_all(send_index.reshape(groups, slots_each), 'grp', split_axis=...  5.58 us
    ppermute x2, starting transfers between devices, with_halo(): lax.ppermute(tail, axis, [(i, (i + 1) % count) for i in range(ends)])  3.84 us
  transfers between devices with their start and end apart: 6, of which 0 were waited for; matrix products, arithmetic and copies ran while one was open for 8% of the time, Pallas kernels for 0%

commit v1 on v0

--- a/solution.py
+++ b/solution.py
@@ -79,7 +79,7 @@
     )
     incoming = with_halo(outgoing, (("col", 0),), RIM)
     edge_in = jnp.concatenate([incoming[:RIM], incoming[3 * RIM :]], axis=0)
-    totals = lax.psum(edge_in, "grp")
+    totals = jnp.sum(lax.all_gather(edge_in, "grp"), axis=0)
     send_rows = (
         jnp.zeros((groups * slots_each, OUTF * NODES), jnp.float32)
         .at[dest]

time: 106 us -> 100 us (0.943)
  blocking collectives: 68.9 us -> 62.7 us
    psum x1 -> x0, blocking collectives: 37.6 us -> none  [local(): totals = lax.psum(edge_in, 'grp')]
    all_gather x0 -> x1, blocking collectives: none -> 31.4 us  [local(): totals = jnp.sum(lax.all_gather(edge_in, 'grp'), axis=0)]
where the time goes in v1:
time: 100 us; the launch traced here: 99.8 us
  blocking collectives  62.7 us (63%)
  starting transfers between devices  22.7 us (23%)
  local copies, waits for them, and re-layouts  8.86 us (9%)
  other arithmetic  2.3 us (2%)
  matrix products  2.29 us (2%)
    all_gather x1, blocking collectives, local(): totals = jnp.sum(lax.all_gather(edge_in, 'grp'), axis=0)  31.4 us
    all_gather x1, blocking collectives, local(): gathered = lax.all_gather(grid_fields, 'grp', axis=0, tiled=True)  31.3 us
    ppermute x2, starting transfers between devices, with_halo(): lax.ppermute(head, axis, [((i + 1) % count, i) for i in range(ends)])  7.28 us
    all_to_all x1, starting transfers between devices, local(): lax.all_to_all(send_rows.reshape(groups, slots_each, OUTF * NODES), 'grp'...  6 us
    all_to_all x1, starting transfers between devices, local(): lax.all_to_all(send_index.reshape(groups, slots_each), 'grp', split_axis=...  5.58 us
    ppermute x2, starting transfers between devices, with_halo(): lax.ppermute(tail, axis, [(i, (i + 1) % count) for i in range(ends)])  3.84 us
    unnamed x15, local copies, waits for them, and re-layouts  2.12 us
  transfers between devices with their start and end apart: 6, of which 0 were waited for; matrix products, arithmetic and copies ran while one was open for 8% of the time, Pallas kernels for 0%

profile of v1, /device:TPU:2, one launch (start us, length us, event | category | flops | bytes accessed | tf_op | source)
XLA Modules:
  0.0 99.8 jit_solution(4209534792258660130)
XLA Ops:
  0.6 0.7 compare_select_fusion
  1.4 31.3 %all_gather.9 = bf16[256,512]{1,0:T(8,128)(2,1)S(1)} all-gather(bf16[32,512]{1,0:T(8,128)(2,1)} %param.10), channel_id=1, replica_groups=mesh['col'=4,'grp'=8] {'grp'}, dimensions={0}, use_global_device_ids=true | all-gather | bytes 294912 | tf_op jit(solution)/shard_map/all_gather | solution.py:53
  32.7 1.2 %gather_fusion = bf16[256,512]{1,0:T(8,128)(2,1)S(1)} fusion(bf16[256,512]{1,0:T(8,128)(2,1)S(1)} %all_gather.9, s32[1024]{0:T(1024)S(1)} %pad_clamp_fusion.3), kind=kCustom, calls=%fused_computation.2 | custom fusion | bytes 525312 | tf_op jit(solution)/shard_map/jit(_take)/gather | solution.py:54
  34.0 1.9 %collective-permute-start = (bf16[16,512]{1,0:T(8,128)(2,1)S(1)}, bf16[16,512]{1,0:T(8,128)(2,1)S(1)}, u32[]{:S(2)}, u32[]{:S(2)}) collective-permute-start(bf16[16,512]{1,0:T(8,128)(2,1)S(1)} %get-tuple-element.17), channel_id=1, source_target_pairs={{0,8},{8,16},{16,24},{1,9},{9,17},{17,25},{2,10},{10,18},{18,26},{... | collective-permute-start | bytes 49160 | tf_op jit(solution)/shard_map/ppermute | solution.py:21
  35.9 3.6 %collective-permute-start.1 = (bf16[16,512]{1,0:T(8,128)(2,1)S(1)}, bf16[16,512]{1,0:T(8,128)(2,1)S(1)}, u32[]{:S(2)}, u32[]{:S(2)}) collective-permute-start(bf16[16,512]{1,0:T(8,128)(2,1)S(1)} %get-tuple-element.18), channel_id=1, source_target_pairs={{8,0},{16,8},{24,16},{9,1},{17,9},{25,17},{10,2},{18,10},{26,18},{... | collective-permute-start | bytes 49160 | tf_op jit(solution)/shard_map/ppermute | solution.py:23
  39.6 0.7 gather_fusion.2
  40.5 0.7 scatter_custom_fusion
  41.2 0.7 all_to_all.9
  41.9 5.6 %all-to-all-start = ((s32[8,1,4]{2,1,0:T(1,128)}), s32[8,1,4]{2,1,0:T(1,128)S(1)}, u32[]{:S(2)}, u32[]{:S(2)}) async-start(s32[8,1,4]{2,1,0:T(1,128)} %bitcast.1), calls=%async_computation | async-start | bytes 8192 | tf_op jit(solution)/shard_map/all_to_all | solution.py:97
  47.5 0.6 copy-done.5
  48.3 0.7 gather_fusion.3
  49.2 0.6 gather_fusion.1
  50.1 0.7 fusion.2
  50.8 0.6 copy-done.1
  52.4 1.9 %collective-permute-start.2 = (f32[16,256]{1,0:T(8,128)S(1)}, f32[16,256]{1,0:T(8,128)S(1)}, u32[]{:S(2)}, u32[]{:S(2)}) collective-permute-start(f32[16,256]{1,0:T(8,128)S(1)} %get-tuple-element.21), channel_id=1, source_target_pairs={{0,8},{8,16},{16,24},{1,9},{9,17},{17,25},{2,10},{10,18},{18,26},{... | collective-permute-start | bytes 49160 | tf_op jit(solution)/shard_map/ppermute | solution.py:21
  54.4 3.6 %collective-permute-start.3 = (f32[16,256]{1,0:T(8,128)S(1)}, f32[16,256]{1,0:T(8,128)S(1)}, u32[]{:S(2)}, u32[]{:S(2)}) collective-permute-start(f32[16,256]{1,0:T(8,128)S(1)} %get-tuple-element.22), channel_id=1, source_target_pairs={{8,0},{16,8},{24,16},{9,1},{17,9},{25,17},{10,2},{18,10},{26,18},{... | collective-permute-start | bytes 49160 | tf_op jit(solution)/shard_map/ppermute | solution.py:23
  58.0 0.5 broadcast.117
  58.6 0.7 reduce.3
  59.3 0.7 scatter_custom_fusion.1
  60.0 0.6 reshape.74
  60.7 6.0 %all-to-all-start.1 = ((f32[8,4,256]{2,1,0:T(4,128)}), f32[8,4,256]{2,1,0:T(4,128)S(1)}, u32[]{:S(2)}, u32[]{:S(2)}) async-start(f32[8,4,256]{2,1,0:T(4,128)} %reshape.74), calls=%async_computation.1 | async-start | bytes 65536 | tf_op jit(solution)/shard_map/all_to_all | solution.py:90
  66.7 0.6 copy.23
  67.3 31.4 %all-gather = f32[256,256]{1,0:T(8,128)S(1)} all-gather(f32[32,256]{1,0:T(8,128)S(1)} %pad_maximum_fusion.1), channel_id=2, replica_groups=mesh['col'=4,'grp'=8] {'grp'}, dimensions={0}, use_global_device_ids=true | all-gather | bytes 294912 | tf_op jit(solution)/shard_map/all_gather | solution.py:82
  98.9 0.9 convolution_add_fusion
  (53 shorter events, 2.2 us)
Async XLA Ops:
  0.6 0.8 copy-start
  34.0 5.6 %copy-start.4 = (s32[32]{0:T(128)S(1)}, s32[32]{0:T(128)}, u32[]{:S(2)}) copy-start(s32[32]{0:T(128)} %param.12) | copy-start | bytes 388
  34.0 15.2 %collective-permute-start = (bf16[16,512]{1,0:T(8,128)(2,1)S(1)}, bf16[16,512]{1,0:T(8,128)(2,1)S(1)}, u32[]{:S(2)}, u32[]{:S(2)}) collective-permute-start(bf16[16,512]{1,0:T(8,128)(2,1)S(1)} %get-tuple-element.17), channel_id=1, source_target_pairs={{0,8},{8,16},{16,24},{1,9},{9,17},{17,25},{2,10},{10,18},{18,26},{... | collective-permute-start | bytes 49160 | tf_op jit(solution)/shard_map/ppermute | solution.py:21
  35.9 13.3 %collective-permute-start.1 = (bf16[16,512]{1,0:T(8,128)(2,1)S(1)}, bf16[16,512]{1,0:T(8,128)(2,1)S(1)}, u32[]{:S(2)}, u32[]{:S(2)}) collective-permute-start(bf16[16,512]{1,0:T(8,128)(2,1)S(1)} %get-tuple-element.18), channel_id=1, source_target_pairs={{8,0},{16,8},{24,16},{9,1},{17,9},{25,17},{10,2},{18,10},{26,18},{... | collective-permute-start | bytes 49160 | tf_op jit(solution)/shard_map/ppermute | solution.py:23
  41.9 16.1 %all-to-all-start = ((s32[8,1,4]{2,1,0:T(1,128)}), s32[8,1,4]{2,1,0:T(1,128)S(1)}, u32[]{:S(2)}, u32[]{:S(2)}) async-start(s32[8,1,4]{2,1,0:T(1,128)} %bitcast.1), calls=%async_computation | async-start | bytes 8192 | tf_op jit(solution)/shard_map/all_to_all | solution.py:97
  47.5 0.7 copy-start.5
  48.3 0.8 copy-start.3
  49.0 1.0 %copy-start.6 = (bf16[32,64,128]{2,1,0:T(8,128)(2,1)S(1)}, bf16[32,64,128]{2,1,0:T(8,128)(2,1)}, u32[]{:S(2)}) copy-start(bf16[32,64,128]{2,1,0:T(8,128)(2,1)} %param.15) | copy-start | bytes 1572868
  50.7 0.7 copy-start.1
  50.8 0.8 copy-start.2
  52.4 14.8 %collective-permute-start.2 = (f32[16,256]{1,0:T(8,128)S(1)}, f32[16,256]{1,0:T(8,128)S(1)}, u32[]{:S(2)}, u32[]{:S(2)}) collective-permute-start(f32[16,256]{1,0:T(8,128)S(1)} %get-tuple-element.21), channel_id=1, source_target_pairs={{0,8},{8,16},{16,24},{1,9},{9,17},{17,25},{2,10},{10,18},{18,26},{... | collective-permute-start | bytes 49160 | tf_op jit(solution)/shard_map/ppermute | solution.py:21
  54.4 12.9 %collective-permute-start.3 = (f32[16,256]{1,0:T(8,128)S(1)}, f32[16,256]{1,0:T(8,128)S(1)}, u32[]{:S(2)}, u32[]{:S(2)}) collective-permute-start(f32[16,256]{1,0:T(8,128)S(1)} %get-tuple-element.22), channel_id=1, source_target_pairs={{8,0},{16,8},{24,16},{9,1},{17,9},{25,17},{10,2},{18,10},{26,18},{... | collective-permute-start | bytes 49160 | tf_op jit(solution)/shard_map/ppermute | solution.py:23
  60.7 38.0 %all-to-all-start.1 = ((f32[8,4,256]{2,1,0:T(4,128)}), f32[8,4,256]{2,1,0:T(4,128)S(1)}, u32[]{:S(2)}, u32[]{:S(2)}) async-start(f32[8,4,256]{2,1,0:T(4,128)} %reshape.74), calls=%async_computation.1 | async-start | bytes 65536 | tf_op jit(solution)/shard_map/all_to_all | solution.py:90
